TPU v7x, 32 devices: a whole 2x2x4 slice. The times are simulated.
32 devices in a mesh: tile: 8 (over z, y), row: 4 (over x, core).
Axes of the slice: x: 2, y: 2, z: 4, core: 2. Of those that a mesh axis runs over, the one named last changes fastest.
Arguments:
- cam_disp: bfloat16 [4, 8, 4, 2, 256, 512], P('row', 'tile')
- footprint: int32 [4, 8, 2, 2], P('row', 'tile'), may hold values from 0 to 15, as said below
- stencil: int32 [4, 8, 2, 2, 2, 256], P('row', 'tile'), may hold values from 0 to 12
- frac: float32 [4, 8, 2, 2, 2, 256], P('row', 'tile'), may hold values from 0 to 1
- coef: float32 [4, 8, 2, 3, 4, 256], P('row', 'tile'), may hold values from -3 to 3
Outputs:
- velocity: bfloat16 [4, 8, 2, 3, 256, 512], P('row', 'tile')
- rfactor: float32 [512, 512], replicated
Inputs may be any that keep to these rules, and one draw needn't show every extreme that they name: `footprint`: for each device, the camera tiles named for camera 0 all lie in one row group and are distinct; those for camera 1 lie in other row groups. So a device needs at most 2 distinct camera tiles from any one row group, and exactly 2 from one of them.
All inputs are finite; a program needn't handle non-finite values.
Results may differ from a plain program's by a relative error of at most 0.0015.
The roundings to bfloat16 on the way count: a program that leaves them out, or rounds other values in their place, can miss the bound.
Values may be sent and summed in bfloat16 or wider, within the bound.
A program may use at most 512 MiB of HBM per device.

v0:
```python
import jax
import jax.numpy as jnp
from jax import lax
from jax.sharding import PartitionSpec as P

TILE_SIDE = 16


def combined_all(array, axis, join):
    gathered = lax.all_gather(array.astype(jnp.bfloat16), axis)

    def take(source):
        return lax.dynamic_index_in_dim(gathered, source, 0, False).astype(array.dtype)

    return lax.fori_loop(
        1, lax.axis_size(axis), lambda source, state: join(state, take(source)), take(0)
    )


def catmull(t):
    k0 = ((-0.5 * t + 1.0) * t - 0.5) * t
    k1 = (1.5 * t - 2.5) * t * t + 1.0
    k2 = ((-1.5 * t + 2.0) * t + 0.5) * t
    k3 = (0.5 * t - 0.5) * t * t
    return (k0, k1, k2, k3)


def axis_weights(base, fraction, side):
    positions = jnp.arange(side, dtype=jnp.int32)
    weights = catmull(fraction)
    total = jnp.zeros(base.shape + (side,), jnp.float32)
    for shift in range(4):
        total = total + weights[shift][..., None] * (positions == base[..., None] + shift).astype(
            jnp.float32
        )
    return total


def combine_factors(first, second):
    stacked = jnp.dot(first.T, first, precision=lax.Precision.HIGHEST) + jnp.dot(
        second.T, second, precision=lax.Precision.HIGHEST
    )
    return jnp.linalg.cholesky(stacked).T


def local(cam_disp, footprint, stencil, frac, coef):
    cam_count = cam_disp.shape[2]
    pix = cam_disp.shape[4]
    snaps = cam_disp.shape[5]
    world = footprint.shape[2]
    cells = coef.shape[-1]
    groups = lax.axis_size("row")
    tiles = cam_disp.reshape(cam_count, 2, pix, snaps)
    ids = footprint.reshape(world * 2)
    pool = lax.all_gather(tiles, "row", axis=0, tiled=True)
    picked = jnp.take(pool, ids, axis=0)
    sten = stencil.reshape(world * 2, 2, cells)
    fraction = frac.reshape(world * 2, 2, cells)
    row_weights = axis_weights(sten[:, 0], fraction[:, 0], TILE_SIDE)
    col_weights = axis_weights(sten[:, 1], fraction[:, 1], TILE_SIDE)
    mats = (
        (row_weights[:, :, :, None] * col_weights[:, :, None, :])
        .reshape(world * 2, cells, pix)
        .astype(jnp.bfloat16)
    )
    interp = jnp.einsum("pqx,pjxs->pjqs", mats, picked, preferred_element_type=jnp.float32)
    interp = interp.reshape(world, 4, cells, snaps)
    weights_coef = coef.reshape(world, 3, 4, cells)
    total = jnp.zeros((world, 3, cells, snaps), jnp.float32)
    for inner in range(4):
        total = total + weights_coef[:, :, inner, :, None] * interp[:, None, inner]
    velocity = total.astype(jnp.bfloat16)
    rows = velocity.reshape(world * 3 * cells, snaps)
    total_rows = groups * lax.axis_size("tile") * world * 3 * cells
    gram_local = lax.dot_general(
        rows, rows, (((0,), (0,)), ((), ())), preferred_element_type=jnp.float32
    ) / jnp.float32(total_rows)
    local_factor = jnp.linalg.cholesky(gram_local).T
    rfactor = combined_all(local_factor, ("tile", "row"), combine_factors)
    return (velocity.reshape(1, 1, world, 3, cells, snaps), rfactor)


def solution(mesh):
    in_specs = (
        P("row", "tile", None, None, None, None),
        P("row", "tile", None, None),
        P("row", "tile", None, None, None, None),
        P("row", "tile", None, None, None, None),
        P("row", "tile", None, None, None, None),
    )
    out_specs = (P("row", "tile", None, None, None, None), P())
    return jax.shard_map(local, mesh=mesh, in_specs=in_specs, out_specs=out_specs, check_vma=False)
```

profile of v0, /device:TPU:0, one launch (start us, length us, event | category | flops | bytes accessed | tf_op | source)
XLA Modules:
  0.0 3035.8 jit_solution(13167744004226206894)
XLA Ops:
  12.3 58.2 %all-gather.5.cloned.1.call-done = bf16[1,1,16,2,256,512]{5,4,3,1,0,2:T(8,128)(2,1)} async-done(((bf16[1,1,4,2,256,512]{5,4,3,1,0,2:T(8,128)(2,1)}), bf16[1,1,16,2,256,512]{5,4,3,1,0,2:T(8,128)(2,1)}) %all-gather.5.cloned.1.call-update) | async-done | bytes 8388624 | tf_op jit(solution)/shard_map/all_gather | solution.py:55
  81.7 11.7 cholesky.358
  106.7 11.9 cholesky.377
  130.7 11.7 cholesky.398
  154.3 12.2 cholesky.415
  178.4 119.4 %all-gather.7.cloned.1.call-done = bf16[16384,512]{0,1:T(8,128)(2,1)} async-done(((bf16[512,512]{0,1:T(8,128)(2,1)}), bf16[16384,512]{0,1:T(8,128)(2,1)}) %all-gather.7.cloned.1.call-update) | async-done | bytes 16777232 | tf_op jit(solution)/shard_map/all_gather | solution.py:10
  298.9 22.5 copy.88
  321.4 2705.8 %while.15 = (s32[]{:T(128)}, f32[512,512]{0,1:T(8,128)S(1)}, bf16[32,512,512]{2,1,0:T(8,128)(2,1)}, s32[]{:T(128)}, s32[]{:T(128)}, /*index=5*/s32[]{:T(128)}, f32[]{:T(128)}) while((s32[]{:T(128)}, f32[512,512]{0,1:T(8,128)S(1)}, bf16[32,512,512]{2,1,0:T(8,128)(2,1)}, s32[]{:T(128)}, s32[]{:T(128)}, /*index=5*/s32[]{:T(128)}, ...), condition=%wide.region_9.11_spmd, body=%wide.region_8.10_spmd.sunk | while | flops 2283667968 | bytes 17043588 | solution.py:15
  325.7 11.7 cholesky.778
  348.1 11.7 cholesky.781
  372.2 11.7 cholesky.783
  395.6 11.7 cholesky.784
  413.0 11.7 cholesky.778
  435.3 11.7 cholesky.781
  459.4 11.7 cholesky.783
  482.9 11.7 cholesky.784
  500.3 11.7 cholesky.778
  522.6 11.7 cholesky.781
  546.7 11.7 cholesky.783
  570.2 11.7 cholesky.784
  657.5 11.7 cholesky.784
  744.8 11.7 cholesky.784
  832.0 11.7 cholesky.784
  919.3 11.7 cholesky.784
  1006.5 11.7 cholesky.784
  1093.8 11.7 cholesky.784
  1181.1 11.7 cholesky.784
  1268.3 11.7 cholesky.784
  1355.6 11.7 cholesky.784
  1443.0 11.7 cholesky.784
  1530.3 11.7 cholesky.784
  1617.6 11.7 cholesky.784
  1704.8 11.7 cholesky.784
  1792.1 11.7 cholesky.784
  1879.4 11.7 cholesky.784
  1966.7 11.7 cholesky.784
  2053.9 11.7 cholesky.784
  2141.2 11.7 cholesky.784
  2228.5 11.7 cholesky.784
  2315.7 11.7 cholesky.784
  2403.0 11.7 cholesky.784
  2490.3 11.7 cholesky.784
  2577.6 11.7 cholesky.784
  2664.8 11.7 cholesky.784
  2752.1 11.7 cholesky.784
  2839.4 11.7 cholesky.784
  2926.8 11.7 cholesky.784
  3014.1 11.7 cholesky.784
  (928 shorter events, 2219.4 us)
Async XLA Ops:
  7.2 63.4 %all-gather.5.cloned.1.call-start = ((), (), s32[]{:S(2)}) async-start(), calls=%async_computation | async-start | bytes 10485760 | tf_op jit(solution)/shard_map/all_gather | solution.py:55
  7.9 289.9 %all-gather.7.cloned.1.call-start = ((), (), s32[]{:S(2)}) async-start(), calls=%async_computation.1 | async-start | bytes 17301504 | tf_op jit(solution)/shard_map/all_gather | solution.py:10
  76.1 1.0 copy-start
  76.1 1.3 copy-start.1
  76.1 1.7 copy-start.2
  80.7 1.0 copy-start.4
  104.1 66.7 %copy-start.3 = (f32[2,256,512]{1,2,0:T(8,128)S(1)}, f32[2,256,512]{1,2,0:T(8,128)}, u32[]{:S(2)}) copy-start(f32[2,256,512]{1,2,0:T(8,128)} %copy-done.2) | copy-start | bytes 3145732
Sparse Core Ops, SparseCore 0:
  9.6 60.9 all-gather.4
  170.8 126.8 all-gather.6
where the time goes:
time: 3050 us; the launch traced here: 3040 us
  other arithmetic  2520 us (83%)
  waiting for transfers between devices  178 us (6%)
  matrix products  178 us (6%)
  loops' own time  83.1 us (3%)
  local copies, waits for them, and re-layouts  54.8 us (2%)
    another operation x434, other arithmetic, combine_factors(): return jnp.linalg.cholesky(stacked).T  2430 us
    all_gather x1, waiting for transfers between devices, combined_all(): gathered = lax.all_gather(array.astype(jnp.bfloat16), axis)  119 us
    another operation x1, loops' own time, combined_all(): lax.fori_loop(1, lax.axis_size(axis), lambda source, state: join(state, t...  83.1 us
    another operation x15, other arithmetic, local(): local_factor = jnp.linalg.cholesky(gram_local).T  79.7 us
  transfers between devices with their start and end apart: 2, of which 2 were waited for; matrix products, arithmetic and copies ran while one was open for 0% of the time, Pallas kernels for 0%

commit v1 on v0

v1 whole, which is shorter than its diff:
```python
import functools

import jax
import jax.numpy as jnp
from jax import lax
from jax.experimental import pallas as pl
from jax.experimental.pallas import tpu as pltpu
from jax.sharding import PartitionSpec as P

TILE_SIDE = 16
BLK = 128
SUB = 8
MESH = pl.DeviceIdType.MESH
VMEM_LIMIT = 48 * 1024 * 1024


def flip(index, bit):
    return index + bit - 2 * bit * (lax.rem(index // bit, 2))


def exchange_kernel(n, count, cam_ref, pool_ref, send_sem, recv_sem, own_sem):
    me = lax.axis_index("row")
    bits = [1 << k for k in range(n.bit_length() - 1)]
    barrier = pltpu.get_barrier_semaphore()
    for bit in bits:
        pl.semaphore_signal(barrier, inc=1, device_id={"row": flip(me, bit)}, device_id_type=MESH)
    pl.semaphore_wait(barrier, len(bits))

    def copy_of(slot, bit, tile):
        src = cam_ref.at[tile] if slot == 0 else pool_ref.at[slot, tile]
        return pltpu.make_async_remote_copy(
            src_ref=src,
            dst_ref=pool_ref.at[slot + bit, tile],
            send_sem=send_sem.at[slot + bit, tile],
            recv_sem=recv_sem.at[slot + bit, tile],
            device_id={"row": flip(me, bit)},
            device_id_type=MESH,
        )

    started = []
    for tile in range(count):
        for bit in reversed(bits):
            c = copy_of(0, bit, tile)
            c.start()
            started.append(c)
    own = pltpu.make_async_copy(cam_ref, pool_ref.at[0], own_sem)
    own.start()
    arrived = set()
    for slot in sorted(range(2, n), key=lambda d: -(d & -d)):
        low = slot & -slot
        if low == 1:
            continue
        for tile in range(count):
            copy_of(slot - low, low, tile).wait_recv()
            arrived.add((slot, tile))
            for bit in bits:
                if bit < low:
                    c = copy_of(slot, bit, tile)
                    c.start()
                    started.append(c)
    for slot in range(1, n):
        low = slot & -slot
        for tile in range(count):
            if (slot, tile) not in arrived:
                copy_of(slot - low, low, tile).wait_recv()
    for c in started:
        c.wait_send()
    own.wait()


def exchange(tiles, n):
    count = tiles.shape[0]
    return pl.pallas_call(
        functools.partial(exchange_kernel, n, count),
        out_shape=jax.ShapeDtypeStruct((n,) + tiles.shape, tiles.dtype),
        in_specs=[pl.BlockSpec(memory_space=pl.ANY)],
        out_specs=pl.BlockSpec(memory_space=pl.ANY),
        scratch_shapes=[
            pltpu.SemaphoreType.DMA((n, count)),
            pltpu.SemaphoreType.DMA((n, count)),
            pltpu.SemaphoreType.DMA,
        ],
        compiler_params=pltpu.CompilerParams(collective_id=0, has_side_effects=True),
        name="camera_exchange",
    )(tiles)


def catmull(t):
    k0 = ((-0.5 * t + 1.0) * t - 0.5) * t
    k1 = (1.5 * t - 2.5) * t * t + 1.0
    k2 = ((-1.5 * t + 2.0) * t + 0.5) * t
    k3 = (0.5 * t - 0.5) * t * t
    return (k0, k1, k2, k3)


def spread(base, weights, positions):
    total = jnp.zeros(positions.shape, jnp.float32)
    for shift in range(4):
        total = jnp.where(positions == base + shift, weights[shift], total)
    return total


def velocity_kernel(ids_ref, *refs):
    first_ref, second_ref, sten_ref, frac_ref, coef_ref, vel_ref, gram_ref = refs
    pix = first_ref.shape[-2]
    snaps = first_ref.shape[-1]
    cells = sten_ref.shape[-1]
    pixel = lax.broadcasted_iota(jnp.int32, (pix, cells), 0)
    prow, pcol = pixel // TILE_SIDE, pixel % TILE_SIDE
    coef = coef_ref[0].T
    interp = []
    for c, tile_ref in enumerate((first_ref, second_ref)):
        sten = sten_ref[0, c]
        frac = frac_ref[0, c]
        rows = spread(sten[0:1], catmull(frac[0:1]), prow)
        cols = spread(sten[1:2], catmull(frac[1:2]), pcol)
        mat = (rows * cols).astype(jnp.bfloat16)
        for j in range(2):
            interp.append(
                lax.dot_general(
                    mat, tile_ref[0, 0, j], (((0,), (0,)), ((), ())), preferred_element_type=jnp.float32
                )
            )
    for k in range(3):
        total = coef[:, 4 * k : 4 * k + 1] * interp[0]
        for i in range(1, 4):
            total = total + coef[:, 4 * k + i : 4 * k + i + 1] * interp[i]
        vel_ref[0, k] = total.astype(jnp.bfloat16)
    rows = vel_ref[0].reshape(3 * cells, snaps)

    @pl.when(pl.program_id(0) == 0)
    def _():
        gram_ref[...] = jnp.zeros_like(gram_ref)

    offset = 0
    for ib in range(snaps // BLK):
        lo = ib * BLK
        width = snaps - lo
        part = lax.dot_general(
            rows[:, lo : lo + BLK], rows[:, lo:], (((0,), (0,)), ((), ())), preferred_element_type=jnp.float32
        )
        for jb in range(width // BLK):
            gram_ref[offset : offset + BLK] += part[:, jb * BLK : (jb + 1) * BLK]
            offset += BLK


def velocity_and_gram(pool, slots, stencil, frac, coef):
    n, count, two, pix, snaps = pool.shape
    world, cells = coef.shape[0], coef.shape[-1]
    nb = snaps // BLK
    packed = nb * (nb + 1) // 2 * BLK

    def tile_spec(c):
        return pl.BlockSpec(
            (1, 1, two, pix, snaps),
            lambda w, ids: (ids[2 * w + c] // count, ids[2 * w + c] % count, 0, 0, 0),
        )

    return pl.pallas_call(
        velocity_kernel,
        grid_spec=pltpu.PrefetchScalarGridSpec(
            num_scalar_prefetch=1,
            grid=(world,),
            in_specs=[
                tile_spec(0),
                tile_spec(1),
                pl.BlockSpec((1, 2, 2, cells), lambda w, ids: (w, 0, 0, 0)),
                pl.BlockSpec((1, 2, 2, cells), lambda w, ids: (w, 0, 0, 0)),
                pl.BlockSpec((1, 12, cells), lambda w, ids: (w, 0, 0)),
            ],
            out_specs=[
                pl.BlockSpec((1, 3, cells, snaps), lambda w, ids: (w, 0, 0, 0)),
                pl.BlockSpec((packed, BLK), lambda w, ids: (0, 0)),
            ],
        ),
        out_shape=[
            jax.ShapeDtypeStruct((world, 3, cells, snaps), jnp.bfloat16),
            jax.ShapeDtypeStruct((packed, BLK), jnp.float32),
        ],
        compiler_params=pltpu.CompilerParams(vmem_limit_bytes=VMEM_LIMIT),
        name="velocity_gram",
    )(slots, pool, pool, stencil, frac, coef.reshape(world, 12, cells))


def sum_phases(rows, n_row, n_tile):
    phases = []
    for size in (2, n_row // 2 * 2, n_tile // 2):
        cut = rows % (size * SUB) == 0
        phases.append((size, rows, cut))
        rows = rows // size if cut else rows
    return phases


def sum_kernel(phases, g_ref, out_ref, acc, *scratch):
    row, tile = lax.axis_index("row"), lax.axis_index("tile")
    row_low, row_high = lax.rem(row, 2), row // 2
    tile_low, tile_high = lax.rem(tile, 2), tile // 2
    ranks = (row_low, row_high * 2 + tile_low, tile_high)
    recv = scratch[: len(phases)]
    send_sem, recv_sem = scratch[len(phases) :]

    def device(phase, rank):
        if phase == 0:
            return (tile, row_high * 2 + rank)
        if phase == 1:
            return (tile_high * 2 + lax.rem(rank, 2), rank // 2 * 2 + row_low)
        return (rank * 2 + tile_low, row)

    barrier = pltpu.get_barrier_semaphore()
    total = 0
    for p, (size, _, _) in enumerate(phases):
        for step in range(1, size):
            peer = lax.rem(ranks[p] + step, size)
            pl.semaphore_signal(barrier, inc=1, device_id=device(p, peer), device_id_type=MESH)
            total += 1
    pl.semaphore_wait(barrier, total)

    sem = 0
    start = 0
    src = g_ref
    starts = []
    for p, (size, rows, cut) in enumerate(phases):
        starts.append(start)
        piece = rows // size if cut else rows
        copies = []
        for step in range(1, size):
            peer = lax.rem(ranks[p] + step, size)
            lo = start + peer * piece if cut else start
            copies.append(
                pltpu.make_async_remote_copy(
                    src_ref=src.at[pl.ds(pl.multiple_of(lo, SUB), piece)],
                    dst_ref=recv[p].at[step - 1],
                    send_sem=send_sem.at[sem],
                    recv_sem=recv_sem.at[sem],
                    device_id=device(p, peer),
                    device_id_type=MESH,
                )
            )
            sem += 1
        for c in copies:
            c.start()
        for c in copies:
            c.wait()
        start = start + ranks[p] * piece if cut else start
        where = pl.ds(pl.multiple_of(start, SUB), piece)
        if cut:
            value = src[where]
            for step in range(1, size):
                value = value + recv[p][step - 1]
        else:
            value = jnp.zeros((piece, BLK), jnp.float32)
            for source in range(size):
                mine = (ranks[p] == source).astype(jnp.float32)
                value = value + src[where] * mine
                for step in range(1, size):
                    theirs = (lax.rem(ranks[p] - step + size, size) == source).astype(jnp.float32)
                    value = value + recv[p][step - 1] * theirs
        last = p == len(phases) - 1
        target = out_ref if last else acc
        target[where] = value
        src = acc

    for p in reversed(range(len(phases))):
        size, rows, cut = phases[p]
        if not cut:
            continue
        piece = rows // size
        where = pl.ds(pl.multiple_of(starts[p] + ranks[p] * piece, SUB), piece)
        copies = []
        for step in range(1, size):
            peer = lax.rem(ranks[p] + step, size)
            copies.append(
                pltpu.make_async_remote_copy(
                    src_ref=out_ref.at[where],
                    dst_ref=out_ref.at[where],
                    send_sem=send_sem.at[sem],
                    recv_sem=recv_sem.at[sem],
                    device_id=device(p, peer),
                    device_id_type=MESH,
                )
            )
            sem += 1
        for c in copies:
            c.start()
        for step, c in enumerate(copies, 1):
            c.wait()


def sum_all(gram, n_row, n_tile):
    phases = sum_phases(gram.shape[0], n_row, n_tile)
    sems = 2 * sum(size - 1 for size, _, _ in phases)
    return pl.pallas_call(
        functools.partial(sum_kernel, phases),
        out_shape=jax.ShapeDtypeStruct(gram.shape, gram.dtype),
        in_specs=[pl.BlockSpec(memory_space=pltpu.VMEM)],
        out_specs=pl.BlockSpec(memory_space=pltpu.VMEM),
        scratch_shapes=[pltpu.VMEM(gram.shape, gram.dtype)]
        + [
            pltpu.VMEM((size - 1, rows // size if cut else rows, BLK), gram.dtype)
            for size, rows, cut in phases
        ]
        + [pltpu.SemaphoreType.DMA((sems,)), pltpu.SemaphoreType.DMA((sems,))],
        compiler_params=pltpu.CompilerParams(
            collective_id=1, has_side_effects=True, vmem_limit_bytes=VMEM_LIMIT
        ),
        name="gram_sum",
    )(gram)


def row_of(x, k):
    return jnp.broadcast_to(x[k : k + 1], x.shape)


def eliminate(panel, out_ref, base, low, step, width):
    r0 = pl.multiple_of(step * SUB, SUB)
    sub = lax.broadcasted_iota(jnp.int32, (SUB, BLK), 0)
    lane = lax.broadcasted_iota(jnp.int32, (SUB, BLK), 1)
    picks = [jnp.full((SUB, BLK), 0, jnp.int32) + (r0 + j) for j in range(SUB)]

    def columns(x):
        return [jnp.take_along_axis(x, picks[j], axis=1, mode="promise_in_bounds") for j in range(SUB)]

    rows = [panel[pl.ds(r0, SUB), b * BLK : (b + 1) * BLK] for b in range(width)]
    cols = columns(rows[0])
    scale = jnp.zeros((SUB, BLK), jnp.float32)
    inverses, heads, tails = [], [], []
    for k in range(SUB):
        root = lax.rsqrt(row_of(cols[k], k))
        inverse = root * root
        scale = jnp.where(sub == k, root, scale)
        head = {j: row_of(cols[j], k) for j in range(k + 1, SUB)}
        tail = [row_of(x, k) for x in rows]
        factor = jnp.where(sub > k, cols[k] * inverse, 0.0)
        for j in range(k + 1, SUB):
            cols[j] = cols[j] - factor * head[j]
        rows = [x - factor * y for x, y in zip(rows, tail)]
        inverses.append(inverse)
        heads.append(head)
        tails.append(tail)
    for b in range(width):
        done = rows[b] * scale
        if b == 0:
            done = jnp.where(lane >= sub + r0, done, 0.0)
        out_ref[pl.ds(pl.multiple_of(base + r0, SUB), SUB), base + b * BLK : base + (b + 1) * BLK] = done
    for i in range(low, BLK // SUB):
        here = pl.ds(i * SUB, SUB)
        other = [panel[here, b * BLK : (b + 1) * BLK] for b in range(width)]
        cols = columns(other[0])
        for k in range(SUB):
            factor = cols[k] * inverses[k]
            for j in range(k + 1, SUB):
                cols[j] = cols[j] - factor * heads[k][j]
            other = [x - factor * y for x, y in zip(other, tails[k])]
        for b in range(width):
            panel[here, b * BLK : (b + 1) * BLK] = other[b]


def factor_kernel(scaling, g_ref, out_ref, *panels):
    nb = len(panels)
    out_ref[...] = jnp.zeros_like(out_ref)
    offset = 0
    for ib in range(nb):
        for jb in range(nb - ib):
            panels[ib][:, jb * BLK : (jb + 1) * BLK] = g_ref[offset : offset + BLK] * scaling
            offset += BLK
    steps = BLK // SUB
    part = 4
    for ib in range(nb):
        base = ib * BLK
        width = nb - ib
        for low in range(0, steps, part):

            def body(step, carry, low=low):
                eliminate(panels[ib], out_ref, base, low, step, width)
                return carry

            lax.fori_loop(low, low + part, body, 0)
        for jb in range(ib + 1, nb):
            left = out_ref[base : base + BLK, jb * BLK : (jb + 1) * BLK]
            right = out_ref[base : base + BLK, jb * BLK :]
            panels[jb][...] -= lax.dot_general(
                left,
                right,
                (((0,), (0,)), ((), ())),
                precision=lax.Precision.HIGHEST,
                preferred_element_type=jnp.float32,
            )


def factor(gram, snaps, total_rows):
    nb = snaps // BLK
    return pl.pallas_call(
        functools.partial(factor_kernel, 1.0 / total_rows),
        out_shape=jax.ShapeDtypeStruct((snaps, snaps), jnp.float32),
        in_specs=[pl.BlockSpec(memory_space=pltpu.VMEM)],
        out_specs=pl.BlockSpec(memory_space=pltpu.VMEM),
        scratch_shapes=[pltpu.VMEM((BLK, (nb - ib) * BLK), jnp.float32) for ib in range(nb)],
        compiler_params=pltpu.CompilerParams(vmem_limit_bytes=VMEM_LIMIT),
        name="cholesky_factor",
    )(gram)


def local(n_row, n_tile, cam_disp, footprint, stencil, frac, coef):
    count, two, pix, snaps = cam_disp.shape[2:]
    world, cells = footprint.shape[2], coef.shape[-1]
    pool = exchange(cam_disp.reshape(count, two, pix, snaps), n_row)
    ids = footprint.reshape(world * 2)
    slots = jnp.bitwise_xor(ids // count, lax.axis_index("row")) * count + ids % count
    velocity, gram = velocity_and_gram(
        pool,
        slots,
        stencil.reshape(world, 2, 2, cells),
        frac.reshape(world, 2, 2, cells),
        coef.reshape(world, 3, 4, cells),
    )
    rfactor = factor(sum_all(gram, n_row, n_tile), snaps, n_row * n_tile * world * 3 * cells)
    return (velocity.reshape(1, 1, world, 3, cells, snaps), rfactor)


def solution(mesh):
    in_specs = (
        P("row", "tile", None, None, None, None),
        P("row", "tile", None, None),
        P("row", "tile", None, None, None, None),
        P("row", "tile", None, None, None, None),
        P("row", "tile", None, None, None, None),
    )
    out_specs = (P("row", "tile", None, None, None, None), P())
    body = functools.partial(local, mesh.shape["row"], mesh.shape["tile"])
    return jax.shard_map(body, mesh=mesh, in_specs=in_specs, out_specs=out_specs, check_vma=False)
```

time: 3050 us -> 122 us (0.04)
  other arithmetic: 2520 us -> 0.02 us
  matrix products: 178 us -> 0 us
  waiting for transfers between devices: 178 us -> 0 us
  Pallas kernels: 0 us -> 120 us
  loops' own time: 83.1 us -> 0 us
  local copies, waits for them, and re-layouts: 54.8 us -> 1.53 us
    another operation x449 -> x0, other arithmetic: 2510 us -> none  [the longest x434 2430 us: combine_factors(): return jnp.linalg.cholesky(stacked).T]
    all_gather x2 -> x0, waiting for transfers between devices: 178 us -> none  [the longest x1 119 us: combined_all(): gathered = lax.all_gather(array.astype(jnp.bfloat16), axis)]
    pallas_call x0 -> x4, Pallas kernels: none -> 120 us  [the longest x1 67.9 us: exchange(): pl.pallas_call(functools.partial(exchange_kernel, n, count), out_shape=ja...]
    dot_general x64 -> x0, matrix products: 114 us -> none  [the longest x31 57.6 us: combine_factors(): jnp.dot(first.T, first, precision=lax.Precision.HIGHEST)]
    another operation x1 -> x0, loops' own time: 83.1 us -> none  [combined_all(): lax.fori_loop(1, lax.axis_size(axis), lambda source, state: join(state, t...]
    another operation x192 -> x0, matrix products: 63.6 us -> none  [the longest x186 58.1 us: combine_factors(): return jnp.linalg.cholesky(stacked).T]
  transfers between devices with their start and end apart: 2 -> 0, of which waited for: 2 -> 0; matrix products, arithmetic and copies ran while one was open for 0% -> 0% of each run, Pallas kernels for 0% -> 0%
where the time goes in v1:
time: 122 us
  Pallas kernels  120 us (98%)
  local copies, waits for them, and re-layouts  1.53 us (1%)
    pallas_call x1, Pallas kernels, exchange(): pl.pallas_call(functools.partial(exchange_kernel, n, count), out_shape=ja...  67.9 us
    pallas_call x1, Pallas kernels, sum_all(): pl.pallas_call(functools.partial(sum_kernel, phases), out_shape=jax.Shape...  24.4 us
    pallas_call x1, Pallas kernels, factor(): pl.pallas_call(functools.partial(factor_kernel, 1.0 / total_rows), out_sh...  22.1 us
    pallas_call x1, Pallas kernels, velocity_and_gram(): pl.pallas_call(velocity_kernel, grid_spec=pltpu.PrefetchScalarGridSpec(nu...  5.46 us

profile of v1, /device:TPU:0, one launch (start us, length us, event | category | flops | bytes accessed | tf_op | source)
XLA Modules:
  0.0 122.0 jit_solution(11960908844887759307)
XLA Ops:
  0.6 0.8 reshape.19
  1.4 0.8 copy.7
  2.2 0.0 copy-start
  2.2 0.0 copy-start.1
  2.2 67.9 %camera_exchange.1.refs_0_.refs_1_ = bf16[4,4,2,256,512]{4,3,2,1,0:T(8,128)(2,1)} custom-call(bf16[4,2,256,512]{3,2,1,0:T(8,128)(2,1)} %bitcast.7), custom_call_target="tpu_custom_call" | custom-call | tf_op jit(solution)/shard_map/camera_exchange/pallas_call | solution.py:73
  70.1 0.0 copy-done
  70.1 0.0 copy-done.1
  70.1 5.5 %velocity_gram.1 = (bf16[2,3,256,512]{3,2,1,0:T(8,128)(2,1)}, f32[1280,128]{1,0:T(8,128)S(1)}) custom-call(s32[4]{0:T(128)S(1)} %fusion.ids_ref, bf16[4,4,2,256,512]{4,3,2,1,0:T(8,128)(2,1)} %camera_exchange.1.refs_0_.refs_1_, bf16[4,4,2,256,512]{4,3,2,1,0:T(8,128)(2,1)} %camera_exchange.1.refs_0_.refs_1_, s32[2,2,2,256]{3,2,1,0:T(2,128)S(1)} %bitcast.5, ...), custom_call_target="tpu_custom_call" | custom-call | tf_op jit(solution)/shard_map/velocity_gram/pallas_call | solution.py:159
  75.6 24.4 %gram_sum.1.g_ref = f32[1280,128]{1,0:T(8,128)S(1)} custom-call(f32[1280,128]{1,0:T(8,128)S(1)} %get-tuple-element.5.g_ref), custom_call_target="tpu_custom_call" | custom-call | tf_op jit(solution)/shard_map/gram_sum/pallas_call | solution.py:292
  100.0 22.1 %cholesky_factor.1 = f32[512,512]{1,0:T(8,128)} custom-call(f32[1280,128]{1,0:T(8,128)S(1)} %gram_sum.1.g_ref), custom_call_target="tpu_custom_call" | custom-call | tf_op jit(solution)/shard_map/cholesky_factor/pallas_call | solution.py:392
  (2 shorter events, 0.0 us)
Async XLA Ops:
  2.2 67.9 %copy-start = (s32[1,1,2,2,2,256]{5,4,3,2,1,0:T(2,128)S(1)}, s32[1,1,2,2,2,256]{5,4,3,2,1,0:T(2,128)}, u32[]{:S(2)}) copy-start(s32[1,1,2,2,2,256]{5,4,3,2,1,0:T(2,128)} %param.7) | copy-start | bytes 24580
  2.2 67.9 %copy-start.1 = (f32[1,1,2,2,2,256]{5,4,3,2,1,0:T(2,128)S(1)}, f32[1,1,2,2,2,256]{5,4,3,2,1,0:T(2,128)}, u32[]{:S(2)}) copy-start(f32[1,1,2,2,2,256]{5,4,3,2,1,0:T(2,128)} %param.8) | copy-start | bytes 24580

commit v2 on v1

--- a/solution.py
+++ b/solution.py
@@ -18,71 +18,102 @@
     return index + bit - 2 * bit * (lax.rem(index // bit, 2))
 
 
-def exchange_kernel(n, count, cam_ref, pool_ref, send_sem, recv_sem, own_sem):
+def exchange_kernel(n, cam_ref, ids_ref, pool_ref, cams, mine, asked, wanted, staged, sems, foot_send, foot_recv, send, recv):
+    _, _, count, two, pix, snaps = cam_ref.shape
+    world = pool_ref.shape[0]
     me = lax.axis_index("row")
-    bits = [1 << k for k in range(n.bit_length() - 1)]
+
+    def peer(d):
+        index = me
+        for k in range(n.bit_length() - 1):
+            if d >> k & 1:
+                index = flip(index, 1 << k)
+        return {"row": index}
+
+    load = pltpu.make_async_copy(cam_ref.at[0, 0], cams, sems.at[0])
+    load.start()
+    line = lax.broadcasted_iota(jnp.int32, mine.shape, 0)
+    filled = jnp.zeros(mine.shape, jnp.int32)
+    for i in range(2 * world):
+        filled = jnp.where(line == i, ids_ref[0, 0, i // 2, i % 2], filled)
+    mine[...] = filled
+    asked[0] = filled
     barrier = pltpu.get_barrier_semaphore()
-    for bit in bits:
-        pl.semaphore_signal(barrier, inc=1, device_id={"row": flip(me, bit)}, device_id_type=MESH)
-    pl.semaphore_wait(barrier, len(bits))
-
-    def copy_of(slot, bit, tile):
-        src = cam_ref.at[tile] if slot == 0 else pool_ref.at[slot, tile]
-        return pltpu.make_async_remote_copy(
-            src_ref=src,
-            dst_ref=pool_ref.at[slot + bit, tile],
-            send_sem=send_sem.at[slot + bit, tile],
-            recv_sem=recv_sem.at[slot + bit, tile],
-            device_id={"row": flip(me, bit)},
+    for d in range(1, n):
+        pl.semaphore_signal(barrier, inc=1, device_id=peer(d), device_id_type=MESH)
+    pl.semaphore_wait(barrier, n - 1)
+
+    requests = [
+        pltpu.make_async_remote_copy(
+            src_ref=mine,
+            dst_ref=asked.at[d],
+            send_sem=foot_send.at[d],
+            recv_sem=foot_recv.at[d],
+            device_id=peer(d),
             device_id_type=MESH,
         )
-
-    started = []
-    for tile in range(count):
-        for bit in reversed(bits):
-            c = copy_of(0, bit, tile)
+        for d in range(1, n)
+    ]
+    for r in requests:
+        r.start()
+    for r in requests:
+        r.wait()
+    known = pltpu.make_async_copy(asked, wanted, sems.at[1])
+    known.start()
+    known.wait()
+    load.wait()
+
+    copies = []
+    order = sorted(range(n), key=lambda d: -d)
+    for w in range(world):
+        for d in order:
+            first, second = wanted[d, 2 * w, 0], wanted[d, 2 * w + 1, 0]
+            here = jnp.where(first // count == me, first % count, second % count)
+            staged[w, d] = cams[here]
+            if d == 0:
+                c = pltpu.make_async_copy(staged.at[w, 0], pool_ref.at[w, 0], sems.at[2 + w])
+            else:
+                c = pltpu.make_async_remote_copy(
+                    src_ref=staged.at[w, d],
+                    dst_ref=pool_ref.at[w, d],
+                    send_sem=send.at[w, d],
+                    recv_sem=recv.at[w, d],
+                    device_id=peer(d),
+                    device_id_type=MESH,
+                )
             c.start()
-            started.append(c)
-    own = pltpu.make_async_copy(cam_ref, pool_ref.at[0], own_sem)
-    own.start()
-    arrived = set()
-    for slot in sorted(range(2, n), key=lambda d: -(d & -d)):
-        low = slot & -slot
-        if low == 1:
-            continue
-        for tile in range(count):
-            copy_of(slot - low, low, tile).wait_recv()
-            arrived.add((slot, tile))
-            for bit in bits:
-                if bit < low:
-                    c = copy_of(slot, bit, tile)
-                    c.start()
-                    started.append(c)
-    for slot in range(1, n):
-        low = slot & -slot
-        for tile in range(count):
-            if (slot, tile) not in arrived:
-                copy_of(slot - low, low, tile).wait_recv()
-    for c in started:
-        c.wait_send()
-    own.wait()
-
-
-def exchange(tiles, n):
-    count = tiles.shape[0]
+            copies.append(c)
+    for c in copies:
+        c.wait()
+
+
+def exchange(cam_disp, footprint, n):
+    _, _, count, two, pix, snaps = cam_disp.shape
+    world = footprint.shape[2]
+    lines = -(-2 * world // SUB) * SUB
+    tile = (two, pix, snaps)
     return pl.pallas_call(
-        functools.partial(exchange_kernel, n, count),
-        out_shape=jax.ShapeDtypeStruct((n,) + tiles.shape, tiles.dtype),
-        in_specs=[pl.BlockSpec(memory_space=pl.ANY)],
+        functools.partial(exchange_kernel, n),
+        out_shape=jax.ShapeDtypeStruct((world, n) + tile, cam_disp.dtype),
+        in_specs=[pl.BlockSpec(memory_space=pl.ANY), pl.BlockSpec(memory_space=pltpu.SMEM)],
         out_specs=pl.BlockSpec(memory_space=pl.ANY),
         scratch_shapes=[
-            pltpu.SemaphoreType.DMA((n, count)),
-            pltpu.SemaphoreType.DMA((n, count)),
-            pltpu.SemaphoreType.DMA,
+            pltpu.VMEM((count,) + tile, cam_disp.dtype),
+            pltpu.VMEM((lines, BLK), jnp.int32),
+            pltpu.VMEM((n, lines, BLK), jnp.int32),
+            pltpu.SMEM((n, lines, BLK), jnp.int32),
+            pltpu.VMEM((world, n) + tile, cam_disp.dtype),
+            pltpu.SemaphoreType.DMA((2 + world,)),
+            pltpu.SemaphoreType.DMA((n,)),
+            pltpu.SemaphoreType.DMA((n,)),
+            pltpu.SemaphoreType.DMA((world, n)),
+            pltpu.SemaphoreType.DMA((world, n)),
         ],
-        compiler_params=pltpu.CompilerParams(collective_id=0, has_side_effects=True),
+        compiler_params=pltpu.CompilerParams(
+            collective_id=0, has_side_effects=True, vmem_limit_bytes=VMEM_LIMIT
+        ),
         name="camera_exchange",
-    )(tiles)
+    )(cam_disp, footprint)
 
 
 def catmull(t):
@@ -100,18 +131,17 @@
     return total
 
 
-def velocity_kernel(ids_ref, *refs):
+def velocity_kernel(ids_ref, me_ref, *refs):
     first_ref, second_ref, sten_ref, frac_ref, coef_ref, vel_ref, gram_ref = refs
     pix = first_ref.shape[-2]
     snaps = first_ref.shape[-1]
     cells = sten_ref.shape[-1]
     pixel = lax.broadcasted_iota(jnp.int32, (pix, cells), 0)
     prow, pcol = pixel // TILE_SIDE, pixel % TILE_SIDE
-    coef = coef_ref[0].T
     interp = []
     for c, tile_ref in enumerate((first_ref, second_ref)):
-        sten = sten_ref[0, c]
-        frac = frac_ref[0, c]
+        sten = sten_ref[0, 0, 0, c]
+        frac = frac_ref[0, 0, 0, c]
         rows = spread(sten[0:1], catmull(frac[0:1]), prow)
         cols = spread(sten[1:2], catmull(frac[1:2]), pcol)
         mat = (rows * cols).astype(jnp.bfloat16)
@@ -122,9 +152,10 @@
                 )
             )
     for k in range(3):
-        total = coef[:, 4 * k : 4 * k + 1] * interp[0]
+        coef = coef_ref[0, 0, 0, k].T
+        total = coef[:, 0:1] * interp[0]
         for i in range(1, 4):
-            total = total + coef[:, 4 * k + i : 4 * k + i + 1] * interp[i]
+            total = total + coef[:, i : i + 1] * interp[i]
         vel_ref[0, k] = total.astype(jnp.bfloat16)
     rows = vel_ref[0].reshape(3 * cells, snaps)
 
@@ -144,33 +175,33 @@
             offset += BLK
 
 
-def velocity_and_gram(pool, slots, stencil, frac, coef):
-    n, count, two, pix, snaps = pool.shape
-    world, cells = coef.shape[0], coef.shape[-1]
+def velocity_and_gram(pool, count, footprint, stencil, frac, coef):
+    _, _, two, pix, snaps = pool.shape
+    world, cells = footprint.shape[2], coef.shape[-1]
     nb = snaps // BLK
     packed = nb * (nb + 1) // 2 * BLK
 
     def tile_spec(c):
         return pl.BlockSpec(
             (1, 1, two, pix, snaps),
-            lambda w, ids: (ids[2 * w + c] // count, ids[2 * w + c] % count, 0, 0, 0),
+            lambda w, ids, me: (w, (ids[0, 0, w, c] // count) ^ me[0], 0, 0, 0),
         )
 
     return pl.pallas_call(
         velocity_kernel,
         grid_spec=pltpu.PrefetchScalarGridSpec(
-            num_scalar_prefetch=1,
+            num_scalar_prefetch=2,
             grid=(world,),
             in_specs=[
                 tile_spec(0),
                 tile_spec(1),
-                pl.BlockSpec((1, 2, 2, cells), lambda w, ids: (w, 0, 0, 0)),
-                pl.BlockSpec((1, 2, 2, cells), lambda w, ids: (w, 0, 0, 0)),
-                pl.BlockSpec((1, 12, cells), lambda w, ids: (w, 0, 0)),
+                pl.BlockSpec((1, 1, 1, 2, 2, cells), lambda w, ids, me: (0, 0, w, 0, 0, 0)),
+                pl.BlockSpec((1, 1, 1, 2, 2, cells), lambda w, ids, me: (0, 0, w, 0, 0, 0)),
+                pl.BlockSpec((1, 1, 1, 3, 4, cells), lambda w, ids, me: (0, 0, w, 0, 0, 0)),
             ],
             out_specs=[
-                pl.BlockSpec((1, 3, cells, snaps), lambda w, ids: (w, 0, 0, 0)),
-                pl.BlockSpec((packed, BLK), lambda w, ids: (0, 0)),
+                pl.BlockSpec((1, 3, cells, snaps), lambda w, ids, me: (w, 0, 0, 0)),
+                pl.BlockSpec((packed, BLK), lambda w, ids, me: (0, 0)),
             ],
         ),
         out_shape=[
@@ -179,7 +210,7 @@
         ],
         compiler_params=pltpu.CompilerParams(vmem_limit_bytes=VMEM_LIMIT),
         name="velocity_gram",
-    )(slots, pool, pool, stencil, frac, coef.reshape(world, 12, cells))
+    )(footprint, lax.axis_index("row").reshape(1), pool, pool, stencil, frac, coef)
 
 
 def sum_phases(rows, n_row, n_tile):
@@ -401,18 +432,10 @@
 
 
 def local(n_row, n_tile, cam_disp, footprint, stencil, frac, coef):
-    count, two, pix, snaps = cam_disp.shape[2:]
+    count, _, _, snaps = cam_disp.shape[2:]
     world, cells = footprint.shape[2], coef.shape[-1]
-    pool = exchange(cam_disp.reshape(count, two, pix, snaps), n_row)
-    ids = footprint.reshape(world * 2)
-    slots = jnp.bitwise_xor(ids // count, lax.axis_index("row")) * count + ids % count
-    velocity, gram = velocity_and_gram(
-        pool,
-        slots,
-        stencil.reshape(world, 2, 2, cells),
-        frac.reshape(world, 2, 2, cells),
-        coef.reshape(world, 3, 4, cells),
-    )
+    pool = exchange(cam_disp, footprint, n_row)
+    velocity, gram = velocity_and_gram(pool, count, footprint, stencil, frac, coef)
     rfactor = factor(sum_all(gram, n_row, n_tile), snaps, n_row * n_tile * world * 3 * cells)
     return (velocity.reshape(1, 1, world, 3, cells, snaps), rfactor)
 

time: 122 us -> 111 us (0.910)
  Pallas kernels: 120 us -> 105 us
  local copies, waits for them, and re-layouts: 1.53 us -> 4.46 us
    pallas_call x1, Pallas kernels: 67.9 us -> 54.4 us  [exchange(): pl.pallas_call(functools.partial(exchange_kernel, n), out_shape=jax.Shape...]
    unnamed x5 -> x14, local copies, waits for them, and re-layouts: 0.76 us -> 4.46 us
where the time goes in v2:
time: 111 us; the launch traced here: 110 us
  Pallas kernels  105 us (95%)
  local copies, waits for them, and re-layouts  4.46 us (4%)
    pallas_call x1, Pallas kernels, exchange(): pl.pallas_call(functools.partial(exchange_kernel, n), out_shape=jax.Shape...  54.4 us
    pallas_call x1, Pallas kernels, sum_all(): pl.pallas_call(functools.partial(sum_kernel, phases), out_shape=jax.Shape...  24.4 us
    pallas_call x1, Pallas kernels, factor(): pl.pallas_call(functools.partial(factor_kernel, 1.0 / total_rows), out_sh...  22.1 us
    unnamed x14, local copies, waits for them, and re-layouts  4.46 us
    pallas_call x1, Pallas kernels, velocity_and_gram(): pl.pallas_call(velocity_kernel, grid_spec=pltpu.PrefetchScalarGridSpec(nu...  4.44 us

profile of v2, /device:TPU:0, one launch (start us, length us, event | category | flops | bytes accessed | tf_op | source)
XLA Modules:
  0.0 110.5 jit_solution(5931054520860319028)
XLA Ops:
  0.6 0.0 copy-start.1
  0.6 1.6 %copy-done.1 = bf16[1,1,4,2,256,512]{5,4,3,2,1,0:T(8,128)(2,1)S(1)} copy-done((bf16[1,1,4,2,256,512]{5,4,3,2,1,0:T(8,128)(2,1)S(1)}, bf16[1,1,4,2,256,512]{5,4,3,2,1,0:T(8,128)(2,1)}, u32[]{:S(2)}) %copy-start.1) | copy-done | bytes 2097176
  2.2 0.0 copy-start.5
  2.2 0.7 copy-done.5
  2.9 0.0 copy-start.2
  2.9 0.0 copy-start.3
  2.9 0.0 copy-start.4
  2.9 0.0 copy-start.6
  2.9 54.4 %camera_exchange.1.refs_0_.refs_1_ = bf16[2,4,2,256,512]{4,3,2,1,0:T(8,128)(2,1)} custom-call(bf16[1,1,4,2,256,512]{5,4,3,2,1,0:T(8,128)(2,1)S(1)} %copy-done.1, s32[1,1,2,2]{3,2,1,0:T(2,128)S(1)} %copy-done.5), custom_call_target="tpu_custom_call" | custom-call | tf_op jit(solution)/shard_map/camera_exchange/pallas_call | solution.py:95
  57.3 0.0 copy-done.2
  57.3 0.0 copy-done.3
  57.3 0.0 copy-done.4
  57.3 0.0 copy-done.6
  57.3 0.0 copy-start
  57.3 2.2 %copy-done = bf16[2,4,2,256,512]{4,3,2,1,0:T(8,128)(2,1)S(1)} copy-done((bf16[2,4,2,256,512]{4,3,2,1,0:T(8,128)(2,1)S(1)}, bf16[2,4,2,256,512]{4,3,2,1,0:T(8,128)(2,1)}, u32[]{:S(2)}) %copy-start) | copy-done | bytes 4194328
  59.5 4.4 %velocity_gram.1 = (bf16[2,3,256,512]{3,2,1,0:T(8,128)(2,1)}, f32[1280,128]{1,0:T(8,128)S(1)}) custom-call(s32[1,1,2,2]{3,2,1,0:T(2,128)S(1)} %copy-done.6, s32[1]{0:T(128)} %bitcast.me_ref, bf16[2,4,2,256,512]{4,3,2,1,0:T(8,128)(2,1)S(1)} %copy-done, bf16[2,4,2,256,512]{4,3,2,1,0:T(8,128)(2,1)S(1)} %copy-done, s32[1,1,2,2,2,256]{5,4,3,2,1,0:T(2,128)S(1)} %copy-done.3, ...), custom_call_target="tpu_custom_call" | custom-call | tf_op jit(solution)/shard_map/velocity_gram/pallas_call | solution.py:190
  64.0 24.4 %gram_sum.1.g_ref = f32[1280,128]{1,0:T(8,128)S(1)} custom-call(f32[1280,128]{1,0:T(8,128)S(1)} %get-tuple-element.5.g_ref), custom_call_target="tpu_custom_call" | custom-call | tf_op jit(solution)/shard_map/gram_sum/pallas_call | solution.py:323
  88.4 22.1 %cholesky_factor.1 = f32[512,512]{1,0:T(8,128)} custom-call(f32[1280,128]{1,0:T(8,128)S(1)} %gram_sum.1.g_ref), custom_call_target="tpu_custom_call" | custom-call | tf_op jit(solution)/shard_map/cholesky_factor/pallas_call | solution.py:423
Async XLA Ops:
  0.6 1.6 %copy-start.1 = (bf16[1,1,4,2,256,512]{5,4,3,2,1,0:T(8,128)(2,1)S(1)}, bf16[1,1,4,2,256,512]{5,4,3,2,1,0:T(8,128)(2,1)}, u32[]{:S(2)}) copy-start(bf16[1,1,4,2,256,512]{5,4,3,2,1,0:T(8,128)(2,1)} %cam_ref.1) | copy-start | bytes 6291460
  2.2 0.7 copy-start.5
  2.9 54.4 %copy-start.2 = (f32[1,1,2,3,4,256]{5,4,3,2,1,0:T(4,128)S(1)}, f32[1,1,2,3,4,256]{5,4,3,2,1,0:T(4,128)}, u32[]{:S(2)}) copy-start(f32[1,1,2,3,4,256]{5,4,3,2,1,0:T(4,128)} %refs_4_.1) | copy-start | bytes 73732
  2.9 54.4 %copy-start.3 = (s32[1,1,2,2,2,256]{5,4,3,2,1,0:T(2,128)S(1)}, s32[1,1,2,2,2,256]{5,4,3,2,1,0:T(2,128)}, u32[]{:S(2)}) copy-start(s32[1,1,2,2,2,256]{5,4,3,2,1,0:T(2,128)} %refs_2_.1) | copy-start | bytes 24580
  2.9 54.4 %copy-start.4 = (f32[1,1,2,2,2,256]{5,4,3,2,1,0:T(2,128)S(1)}, f32[1,1,2,2,2,256]{5,4,3,2,1,0:T(2,128)}, u32[]{:S(2)}) copy-start(f32[1,1,2,2,2,256]{5,4,3,2,1,0:T(2,128)} %refs_3_.1) | copy-start | bytes 24580
  2.9 54.4 %copy-start.6 = (s32[1,1,2,2]{3,2,1,0:T(2,128)S(1)}, s32[1,1,2,2]{3,2,1,0:T(2,128)}, u32[]{:S(2)}) copy-start(s32[1,1,2,2]{3,2,1,0:T(2,128)} %ids_ref.3) | copy-start | bytes 52
  57.3 2.2 %copy-start = (bf16[2,4,2,256,512]{4,3,2,1,0:T(8,128)(2,1)S(1)}, bf16[2,4,2,256,512]{4,3,2,1,0:T(8,128)(2,1)}, u32[]{:S(2)}) copy-start(bf16[2,4,2,256,512]{4,3,2,1,0:T(8,128)(2,1)} %camera_exchange.1.refs_0_.refs_1_) | copy-start | bytes 12582916

commit v3 on v2

--- a/solution.py
+++ b/solution.py
@@ -342,17 +342,15 @@
     return jnp.broadcast_to(x[k : k + 1], x.shape)
 
 
-def eliminate(panel, out_ref, base, low, step, width):
-    r0 = pl.multiple_of(step * SUB, SUB)
+def columns(x, r0):
+    return [jnp.broadcast_to(x[:, r0 + j : r0 + j + 1], x.shape) for j in range(SUB)]
+
+
+def eliminate(panel, out_ref, base, step, width, rows):
+    r0 = step * SUB
     sub = lax.broadcasted_iota(jnp.int32, (SUB, BLK), 0)
     lane = lax.broadcasted_iota(jnp.int32, (SUB, BLK), 1)
-    picks = [jnp.full((SUB, BLK), 0, jnp.int32) + (r0 + j) for j in range(SUB)]
-
-    def columns(x):
-        return [jnp.take_along_axis(x, picks[j], axis=1, mode="promise_in_bounds") for j in range(SUB)]
-
-    rows = [panel[pl.ds(r0, SUB), b * BLK : (b + 1) * BLK] for b in range(width)]
-    cols = columns(rows[0])
+    cols = columns(rows[0], r0)
     scale = jnp.zeros((SUB, BLK), jnp.float32)
     inverses, heads, tails = [], [], []
     for k in range(SUB):
@@ -372,18 +370,23 @@
         done = rows[b] * scale
         if b == 0:
             done = jnp.where(lane >= sub + r0, done, 0.0)
-        out_ref[pl.ds(pl.multiple_of(base + r0, SUB), SUB), base + b * BLK : base + (b + 1) * BLK] = done
-    for i in range(low, BLK // SUB):
-        here = pl.ds(i * SUB, SUB)
+        out_ref[base + r0 : base + r0 + SUB, base + b * BLK : base + (b + 1) * BLK] = done
+    following = None
+    for i in range(step + 1, BLK // SUB):
+        here = slice(i * SUB, (i + 1) * SUB)
         other = [panel[here, b * BLK : (b + 1) * BLK] for b in range(width)]
-        cols = columns(other[0])
+        cols = columns(other[0], r0)
         for k in range(SUB):
             factor = cols[k] * inverses[k]
             for j in range(k + 1, SUB):
                 cols[j] = cols[j] - factor * heads[k][j]
             other = [x - factor * y for x, y in zip(other, tails[k])]
-        for b in range(width):
-            panel[here, b * BLK : (b + 1) * BLK] = other[b]
+        if following is None:
+            following = other
+        else:
+            for b in range(width):
+                panel[here, b * BLK : (b + 1) * BLK] = other[b]
+    return following
 
 
 def factor_kernel(scaling, g_ref, out_ref, *panels):
@@ -394,18 +397,12 @@
         for jb in range(nb - ib):
             panels[ib][:, jb * BLK : (jb + 1) * BLK] = g_ref[offset : offset + BLK] * scaling
             offset += BLK
-    steps = BLK // SUB
-    part = 4
     for ib in range(nb):
         base = ib * BLK
         width = nb - ib
-        for low in range(0, steps, part):
-
-            def body(step, carry, low=low):
-                eliminate(panels[ib], out_ref, base, low, step, width)
-                return carry
-
-            lax.fori_loop(low, low + part, body, 0)
+        rows = [panels[ib][0:SUB, b * BLK : (b + 1) * BLK] for b in range(width)]
+        for step in range(BLK // SUB):
+            rows = eliminate(panels[ib], out_ref, base, step, width, rows)
         for jb in range(ib + 1, nb):
             left = out_ref[base : base + BLK, jb * BLK : (jb + 1) * BLK]
             right = out_ref[base : base + BLK, jb * BLK :]

time: 111 us -> 108 us (0.973)
  Pallas kernels: 105 us -> 102 us
    pallas_call x1, Pallas kernels: 22.1 us -> 19.2 us  [factor(): pl.pallas_call(functools.partial(factor_kernel, 1.0 / total_rows), out_sh...]
where the time goes in v3:
time: 108 us
  Pallas kernels  102 us (94%)
  local copies, waits for them, and re-layouts  4.46 us (4%)
    pallas_call x1, Pallas kernels, exchange(): pl.pallas_call(functools.partial(exchange_kernel, n), out_shape=jax.Shape...  54.4 us
    pallas_call x1, Pallas kernels, sum_all(): pl.pallas_call(functools.partial(sum_kernel, phases), out_shape=jax.Shape...  24.4 us
    pallas_call x1, Pallas kernels, factor(): pl.pallas_call(functools.partial(factor_kernel, 1.0 / total_rows), out_sh...  19.2 us
    unnamed x14, local copies, waits for them, and re-layouts  4.46 us
    pallas_call x1, Pallas kernels, velocity_and_gram(): pl.pallas_call(velocity_kernel, grid_spec=pltpu.PrefetchScalarGridSpec(nu...  4.43 us

profile of v3, /device:TPU:0, one launch (start us, length us, event | category | flops | bytes accessed | tf_op | source)
XLA Modules:
  0.0 107.5 jit_solution(1513255371375766776)
XLA Ops:
  0.6 0.0 copy-start.1
  0.6 1.6 %copy-done.1 = bf16[1,1,4,2,256,512]{5,4,3,2,1,0:T(8,128)(2,1)S(1)} copy-done((bf16[1,1,4,2,256,512]{5,4,3,2,1,0:T(8,128)(2,1)S(1)}, bf16[1,1,4,2,256,512]{5,4,3,2,1,0:T(8,128)(2,1)}, u32[]{:S(2)}) %copy-start.1) | copy-done | bytes 2097176
  2.2 0.0 copy-start.5
  2.2 0.7 copy-done.5
  2.9 0.0 copy-start.2
  2.9 0.0 copy-start.3
  2.9 0.0 copy-start.4
  2.9 0.0 copy-start.6
  2.9 54.4 %camera_exchange.1.refs_0_.refs_1_ = bf16[2,4,2,256,512]{4,3,2,1,0:T(8,128)(2,1)} custom-call(bf16[1,1,4,2,256,512]{5,4,3,2,1,0:T(8,128)(2,1)S(1)} %copy-done.1, s32[1,1,2,2]{3,2,1,0:T(2,128)S(1)} %copy-done.5), custom_call_target="tpu_custom_call" | custom-call | tf_op jit(solution)/shard_map/camera_exchange/pallas_call | solution.py:95
  57.3 0.0 copy-done.2
  57.3 0.0 copy-done.3
  57.3 0.0 copy-done.4
  57.3 0.0 copy-done.6
  57.3 0.0 copy-start
  57.3 2.2 %copy-done = bf16[2,4,2,256,512]{4,3,2,1,0:T(8,128)(2,1)S(1)} copy-done((bf16[2,4,2,256,512]{4,3,2,1,0:T(8,128)(2,1)S(1)}, bf16[2,4,2,256,512]{4,3,2,1,0:T(8,128)(2,1)}, u32[]{:S(2)}) %copy-start) | copy-done | bytes 4194328
  59.5 4.4 %velocity_gram.1 = (bf16[2,3,256,512]{3,2,1,0:T(8,128)(2,1)}, f32[1280,128]{1,0:T(8,128)S(1)}) custom-call(s32[1,1,2,2]{3,2,1,0:T(2,128)S(1)} %copy-done.6, s32[1]{0:T(128)} %bitcast.me_ref, bf16[2,4,2,256,512]{4,3,2,1,0:T(8,128)(2,1)S(1)} %copy-done, bf16[2,4,2,256,512]{4,3,2,1,0:T(8,128)(2,1)S(1)} %copy-done, s32[1,1,2,2,2,256]{5,4,3,2,1,0:T(2,128)S(1)} %copy-done.3, ...), custom_call_target="tpu_custom_call" | custom-call | tf_op jit(solution)/shard_map/velocity_gram/pallas_call | solution.py:190
  64.0 24.4 %gram_sum.1.g_ref = f32[1280,128]{1,0:T(8,128)S(1)} custom-call(f32[1280,128]{1,0:T(8,128)S(1)} %get-tuple-element.5.g_ref), custom_call_target="tpu_custom_call" | custom-call | tf_op jit(solution)/shard_map/gram_sum/pallas_call | solution.py:323
  88.4 19.2 %cholesky_factor.1 = f32[512,512]{1,0:T(8,128)} custom-call(f32[1280,128]{1,0:T(8,128)S(1)} %gram_sum.1.g_ref), custom_call_target="tpu_custom_call" | custom-call | tf_op jit(solution)/shard_map/cholesky_factor/pallas_call | solution.py:420
Async XLA Ops:
  0.6 1.6 %copy-start.1 = (bf16[1,1,4,2,256,512]{5,4,3,2,1,0:T(8,128)(2,1)S(1)}, bf16[1,1,4,2,256,512]{5,4,3,2,1,0:T(8,128)(2,1)}, u32[]{:S(2)}) copy-start(bf16[1,1,4,2,256,512]{5,4,3,2,1,0:T(8,128)(2,1)} %cam_ref.1) | copy-start | bytes 6291460
  2.2 0.7 copy-start.5
  2.9 54.4 %copy-start.2 = (f32[1,1,2,3,4,256]{5,4,3,2,1,0:T(4,128)S(1)}, f32[1,1,2,3,4,256]{5,4,3,2,1,0:T(4,128)}, u32[]{:S(2)}) copy-start(f32[1,1,2,3,4,256]{5,4,3,2,1,0:T(4,128)} %refs_4_.1) | copy-start | bytes 73732
  2.9 54.4 %copy-start.3 = (s32[1,1,2,2,2,256]{5,4,3,2,1,0:T(2,128)S(1)}, s32[1,1,2,2,2,256]{5,4,3,2,1,0:T(2,128)}, u32[]{:S(2)}) copy-start(s32[1,1,2,2,2,256]{5,4,3,2,1,0:T(2,128)} %refs_2_.1) | copy-start | bytes 24580
  2.9 54.4 %copy-start.4 = (f32[1,1,2,2,2,256]{5,4,3,2,1,0:T(2,128)S(1)}, f32[1,1,2,2,2,256]{5,4,3,2,1,0:T(2,128)}, u32[]{:S(2)}) copy-start(f32[1,1,2,2,2,256]{5,4,3,2,1,0:T(2,128)} %refs_3_.1) | copy-start | bytes 24580
  2.9 54.4 %copy-start.6 = (s32[1,1,2,2]{3,2,1,0:T(2,128)S(1)}, s32[1,1,2,2]{3,2,1,0:T(2,128)}, u32[]{:S(2)}) copy-start(s32[1,1,2,2]{3,2,1,0:T(2,128)} %ids_ref.3) | copy-start | bytes 52
  57.3 2.2 %copy-start = (bf16[2,4,2,256,512]{4,3,2,1,0:T(8,128)(2,1)S(1)}, bf16[2,4,2,256,512]{4,3,2,1,0:T(8,128)(2,1)}, u32[]{:S(2)}) copy-start(bf16[2,4,2,256,512]{4,3,2,1,0:T(8,128)(2,1)} %camera_exchange.1.refs_0_.refs_1_) | copy-start | bytes 12582916

commit v4 on v3

--- a/solution.py
+++ b/solution.py
@@ -12,15 +12,18 @@
 SUB = 8
 MESH = pl.DeviceIdType.MESH
 VMEM_LIMIT = 48 * 1024 * 1024
+VMEM_MOST = 60 * 1024 * 1024
 
 
 def flip(index, bit):
     return index + bit - 2 * bit * (lax.rem(index // bit, 2))
 
 
-def exchange_kernel(n, cam_ref, ids_ref, pool_ref, cams, mine, asked, wanted, staged, sems, foot_send, foot_recv, send, recv):
+def velocity_kernel(n, cam_ref, ids_ref, sten_ref, frac_ref, coef_ref, vel_ref, gram_ref, *scratch):
     _, _, count, two, pix, snaps = cam_ref.shape
-    world = pool_ref.shape[0]
+    world = vel_ref.shape[0]
+    pools = scratch[:world]
+    cams, mats, mine, asked, wanted, staged, sems, foot_send, foot_recv, send, recv = scratch[world:]
     me = lax.axis_index("row")
 
     def peer(d):
@@ -69,51 +72,39 @@
         for d in order:
             first, second = wanted[d, 2 * w, 0], wanted[d, 2 * w + 1, 0]
             here = jnp.where(first // count == me, first % count, second % count)
+            if d == 0:
+                pools[w][0] = cams[here]
+                continue
             staged[w, d] = cams[here]
-            if d == 0:
-                c = pltpu.make_async_copy(staged.at[w, 0], pool_ref.at[w, 0], sems.at[2 + w])
-            else:
-                c = pltpu.make_async_remote_copy(
-                    src_ref=staged.at[w, d],
-                    dst_ref=pool_ref.at[w, d],
-                    send_sem=send.at[w, d],
-                    recv_sem=recv.at[w, d],
-                    device_id=peer(d),
-                    device_id_type=MESH,
-                )
+            c = pltpu.make_async_remote_copy(
+                src_ref=staged.at[w, d],
+                dst_ref=pools[w].at[d],
+                send_sem=send.at[w, d],
+                recv_sem=recv.at[w, d],
+                device_id=peer(d),
+                device_id_type=MESH,
+            )
             c.start()
-            copies.append(c)
-    for c in copies:
-        c.wait()
-
-
-def exchange(cam_disp, footprint, n):
-    _, _, count, two, pix, snaps = cam_disp.shape
-    world = footprint.shape[2]
-    lines = -(-2 * world // SUB) * SUB
-    tile = (two, pix, snaps)
-    return pl.pallas_call(
-        functools.partial(exchange_kernel, n),
-        out_shape=jax.ShapeDtypeStruct((world, n) + tile, cam_disp.dtype),
-        in_specs=[pl.BlockSpec(memory_space=pl.ANY), pl.BlockSpec(memory_space=pltpu.SMEM)],
-        out_specs=pl.BlockSpec(memory_space=pl.ANY),
-        scratch_shapes=[
-            pltpu.VMEM((count,) + tile, cam_disp.dtype),
-            pltpu.VMEM((lines, BLK), jnp.int32),
-            pltpu.VMEM((n, lines, BLK), jnp.int32),
-            pltpu.SMEM((n, lines, BLK), jnp.int32),
-            pltpu.VMEM((world, n) + tile, cam_disp.dtype),
-            pltpu.SemaphoreType.DMA((2 + world,)),
-            pltpu.SemaphoreType.DMA((n,)),
-            pltpu.SemaphoreType.DMA((n,)),
-            pltpu.SemaphoreType.DMA((world, n)),
-            pltpu.SemaphoreType.DMA((world, n)),
-        ],
-        compiler_params=pltpu.CompilerParams(
-            collective_id=0, has_side_effects=True, vmem_limit_bytes=VMEM_LIMIT
-        ),
-        name="camera_exchange",
-    )(cam_disp, footprint)
+            copies.append((w, c))
+    for w in range(world):
+        for c in range(2):
+            mats[2 * w + c] = interp_matrix(sten_ref[0, 0, w, c], frac_ref[0, 0, w, c], pix)
+    gram_ref[...] = jnp.zeros_like(gram_ref)
+    for w in range(world):
+        for owner, c in copies:
+            if owner == w:
+                c.wait_recv()
+        tiles = []
+        for c in range(2):
+            group = ids_ref[0, 0, w, c] // count
+            slot = 0
+            for k in range(n.bit_length() - 1):
+                bit = 1 << k
+                slot = slot + bit * lax.rem(group // bit + me // bit, 2)
+            tiles.append(pools[w][slot])
+        velocity_of(w, mats, tiles, coef_ref, vel_ref, gram_ref)
+    for _, c in copies:
+        c.wait_send()
 
 
 def catmull(t):
@@ -131,38 +122,29 @@
     return total
 
 
-def velocity_kernel(ids_ref, me_ref, *refs):
-    first_ref, second_ref, sten_ref, frac_ref, coef_ref, vel_ref, gram_ref = refs
-    pix = first_ref.shape[-2]
-    snaps = first_ref.shape[-1]
-    cells = sten_ref.shape[-1]
-    pixel = lax.broadcasted_iota(jnp.int32, (pix, cells), 0)
-    prow, pcol = pixel // TILE_SIDE, pixel % TILE_SIDE
-    interp = []
-    for c, tile_ref in enumerate((first_ref, second_ref)):
-        sten = sten_ref[0, 0, 0, c]
-        frac = frac_ref[0, 0, 0, c]
-        rows = spread(sten[0:1], catmull(frac[0:1]), prow)
-        cols = spread(sten[1:2], catmull(frac[1:2]), pcol)
-        mat = (rows * cols).astype(jnp.bfloat16)
-        for j in range(2):
-            interp.append(
-                lax.dot_general(
-                    mat, tile_ref[0, 0, j], (((0,), (0,)), ((), ())), preferred_element_type=jnp.float32
-                )
-            )
+def interp_matrix(sten, frac, pix):
+    pixel = lax.broadcasted_iota(jnp.int32, (pix, sten.shape[-1]), 0)
+    rows = spread(sten[0:1], catmull(frac[0:1]), pixel // TILE_SIDE)
+    cols = spread(sten[1:2], catmull(frac[1:2]), pixel % TILE_SIDE)
+    return (rows * cols).astype(jnp.bfloat16)
+
+
+def velocity_of(w, mats, tiles, coef_ref, vel_ref, gram_ref):
+    _, _, cells, snaps = vel_ref.shape
+    interp = [
+        lax.dot_general(
+            mats[2 * w + c], tiles[c][j], (((0,), (0,)), ((), ())), preferred_element_type=jnp.float32
+        )
+        for c in range(2)
+        for j in range(2)
+    ]
     for k in range(3):
-        coef = coef_ref[0, 0, 0, k].T
+        coef = coef_ref[0, 0, w, k].T
         total = coef[:, 0:1] * interp[0]
         for i in range(1, 4):
             total = total + coef[:, i : i + 1] * interp[i]
-        vel_ref[0, k] = total.astype(jnp.bfloat16)
-    rows = vel_ref[0].reshape(3 * cells, snaps)
-
-    @pl.when(pl.program_id(0) == 0)
-    def _():
-        gram_ref[...] = jnp.zeros_like(gram_ref)
-
+        vel_ref[w, k] = total.astype(jnp.bfloat16)
+    rows = vel_ref[w].reshape(3 * cells, snaps)
     offset = 0
     for ib in range(snaps // BLK):
         lo = ib * BLK
@@ -175,42 +157,47 @@
             offset += BLK
 
 
-def velocity_and_gram(pool, count, footprint, stencil, frac, coef):
-    _, _, two, pix, snaps = pool.shape
+def velocity_and_gram(cam_disp, footprint, stencil, frac, coef, n):
+    _, _, count, two, pix, snaps = cam_disp.shape
     world, cells = footprint.shape[2], coef.shape[-1]
     nb = snaps // BLK
     packed = nb * (nb + 1) // 2 * BLK
-
-    def tile_spec(c):
-        return pl.BlockSpec(
-            (1, 1, two, pix, snaps),
-            lambda w, ids, me: (w, (ids[0, 0, w, c] // count) ^ me[0], 0, 0, 0),
-        )
-
+    lines = -(-2 * world // SUB) * SUB
+    tile = (two, pix, snaps)
+    vmem = pl.BlockSpec(memory_space=pltpu.VMEM)
     return pl.pallas_call(
-        velocity_kernel,
-        grid_spec=pltpu.PrefetchScalarGridSpec(
-            num_scalar_prefetch=2,
-            grid=(world,),
-            in_specs=[
-                tile_spec(0),
-                tile_spec(1),
-                pl.BlockSpec((1, 1, 1, 2, 2, cells), lambda w, ids, me: (0, 0, w, 0, 0, 0)),
-                pl.BlockSpec((1, 1, 1, 2, 2, cells), lambda w, ids, me: (0, 0, w, 0, 0, 0)),
-                pl.BlockSpec((1, 1, 1, 3, 4, cells), lambda w, ids, me: (0, 0, w, 0, 0, 0)),
-            ],
-            out_specs=[
-                pl.BlockSpec((1, 3, cells, snaps), lambda w, ids, me: (w, 0, 0, 0)),
-                pl.BlockSpec((packed, BLK), lambda w, ids, me: (0, 0)),
-            ],
-        ),
+        functools.partial(velocity_kernel, n),
         out_shape=[
             jax.ShapeDtypeStruct((world, 3, cells, snaps), jnp.bfloat16),
             jax.ShapeDtypeStruct((packed, BLK), jnp.float32),
         ],
-        compiler_params=pltpu.CompilerParams(vmem_limit_bytes=VMEM_LIMIT),
+        in_specs=[
+            pl.BlockSpec(memory_space=pl.ANY),
+            pl.BlockSpec(memory_space=pltpu.SMEM),
+            vmem,
+            vmem,
+            vmem,
+        ],
+        out_specs=[vmem, vmem],
+        scratch_shapes=[pltpu.VMEM((n,) + tile, cam_disp.dtype) for _ in range(world)]
+        + [
+            pltpu.VMEM((count,) + tile, cam_disp.dtype),
+            pltpu.VMEM((2 * world, pix, cells), jnp.bfloat16),
+            pltpu.VMEM((lines, BLK), jnp.int32),
+            pltpu.VMEM((n, lines, BLK), jnp.int32),
+            pltpu.SMEM((n, lines, BLK), jnp.int32),
+            pltpu.VMEM((world, n) + tile, cam_disp.dtype),
+            pltpu.SemaphoreType.DMA((2,)),
+            pltpu.SemaphoreType.DMA((n,)),
+            pltpu.SemaphoreType.DMA((n,)),
+            pltpu.SemaphoreType.DMA((world, n)),
+            pltpu.SemaphoreType.DMA((world, n)),
+        ],
+        compiler_params=pltpu.CompilerParams(
+            collective_id=0, has_side_effects=True, vmem_limit_bytes=VMEM_MOST
+        ),
         name="velocity_gram",
-    )(footprint, lax.axis_index("row").reshape(1), pool, pool, stencil, frac, coef)
+    )(cam_disp, footprint, stencil, frac, coef)
 
 
 def sum_phases(rows, n_row, n_tile):
@@ -429,10 +416,9 @@
 
 
 def local(n_row, n_tile, cam_disp, footprint, stencil, frac, coef):
-    count, _, _, snaps = cam_disp.shape[2:]
+    snaps = cam_disp.shape[-1]
     world, cells = footprint.shape[2], coef.shape[-1]
-    pool = exchange(cam_disp, footprint, n_row)
-    velocity, gram = velocity_and_gram(pool, count, footprint, stencil, frac, coef)
+    velocity, gram = velocity_and_gram(cam_disp, footprint, stencil, frac, coef, n_row)
     rfactor = factor(sum_all(gram, n_row, n_tile), snaps, n_row * n_tile * world * 3 * cells)
     return (velocity.reshape(1, 1, world, 3, cells, snaps), rfactor)
 

time: 108 us -> 104 us (0.963)
  local copies, waits for them, and re-layouts: 4.46 us -> 2.23 us
    unnamed x14 -> x5, local copies, waits for them, and re-layouts: 4.46 us -> 2.23 us
    pallas_call x2 -> x1, Pallas kernels: 58.8 us -> 57.3 us  [velocity_and_gram(): pl.pallas_call(functools.partial(velocity_kernel, n), out_shape=[jax.Shap...]
where the time goes in v4:
time: 104 us
  Pallas kernels  101 us (97%)
  local copies, waits for them, and re-layouts  2.23 us (2%)
    pallas_call x1, Pallas kernels, velocity_and_gram(): pl.pallas_call(functools.partial(velocity_kernel, n), out_shape=[jax.Shap...  57.3 us
    pallas_call x1, Pallas kernels, sum_all(): pl.pallas_call(functools.partial(sum_kernel, phases), out_shape=jax.Shape...  24.4 us
    pallas_call x1, Pallas kernels, factor(): pl.pallas_call(functools.partial(factor_kernel, 1.0 / total_rows), out_sh...  19.1 us
    unnamed x5, local copies, waits for them, and re-layouts  2.23 us

profile of v4, /device:TPU:0, one launch (start us, length us, event | category | flops | bytes accessed | tf_op | source)
XLA Modules:
  0.0 103.6 jit_solution(10853237837602741769)
XLA Ops:
  0.6 57.3 %velocity_gram.1 = (bf16[2,3,256,512]{3,2,1,0:T(8,128)(2,1)}, f32[1280,128]{1,0:T(8,128)}) custom-call(bf16[1,1,4,2,256,512]{5,4,3,2,1,0:T(8,128)(2,1)} %cam_ref.1, s32[1,1,2,2]{3,2,1,0:T(2,128)} %ids_ref.1, s32[1,1,2,2,2,256]{5,4,3,2,1,0:T(2,128)} %sten_ref.1, f32[1,1,2,2,2,256]{5,4,3,2,1,0:T(2,128)} %frac_ref.1, f32[1,1,2,3,4,256]{5,4,3,2,1,0:T(4,128)} %coef_ref.1), custom_call_target="tpu_custom_call" | custom-call | tf_op jit(solution)/shard_map/velocity_gram/pallas_call | solution.py:168
  57.9 0.0 copy-start
  57.9 1.1 %copy-done = f32[1280,128]{1,0:T(8,128)S(1)} copy-done((f32[1280,128]{1,0:T(8,128)S(1)}, f32[1280,128]{1,0:T(8,128)}, u32[]{:S(2)}) %copy-start) | copy-done | bytes 655384
  59.0 0.0 copy-start.1
  59.0 24.4 %gram_sum.1.g_ref = f32[1280,128]{1,0:T(8,128)S(1)} custom-call(f32[1280,128]{1,0:T(8,128)S(1)} %copy-done), custom_call_target="tpu_custom_call" | custom-call | tf_op jit(solution)/shard_map/gram_sum/pallas_call | solution.py:310
  83.4 19.1 %cholesky_factor.1 = f32[512,512]{1,0:T(8,128)} custom-call(f32[1280,128]{1,0:T(8,128)S(1)} %gram_sum.1.g_ref), custom_call_target="tpu_custom_call" | custom-call | tf_op jit(solution)/shard_map/cholesky_factor/pallas_call | solution.py:407
  102.5 0.0 copy-done.1
  102.5 1.1 %copy.8 = bf16[1,1,2,3,256,512]{5,4,3,2,1,0:T(8,128)(2,1)} copy(bf16[1,1,2,3,256,512]{5,4,3,2,1,0:T(8,128)(2,1)S(1)} %bitcast.1) | data formatting | bytes 3145728
Async XLA Ops:
  57.9 1.1 %copy-start = (f32[1280,128]{1,0:T(8,128)S(1)}, f32[1280,128]{1,0:T(8,128)}, u32[]{:S(2)}) copy-start(f32[1280,128]{1,0:T(8,128)} %get-tuple-element.5.g_ref) | copy-start | bytes 1966084
  59.0 43.5 %copy-start.1 = (bf16[2,3,256,512]{3,2,1,0:T(8,128)(2,1)S(1)}, bf16[2,3,256,512]{3,2,1,0:T(8,128)(2,1)}, u32[]{:S(2)}) copy-start(bf16[2,3,256,512]{3,2,1,0:T(8,128)(2,1)} %get-tuple-element.4) | copy-start | bytes 4718596
